TPU v7x, 32 devices: a whole 2x2x4 slice. The times are simulated.
32 devices in a mesh: groups: 2 (over y), owner: 16 (over z, x, core).
Axes of the slice: x: 2, y: 2, z: 4, core: 2. Of those that a mesh axis runs over, the one named last changes fastest.
Arguments:
- token_input_rows: bfloat16 [4096, 4096], P(('groups', 'owner')), parts along dimension 0, may hold values from -6 to 6
- output_gradient_rows: bfloat16 [4096, 1024], P(('groups', 'owner')), parts along dimension 0, may hold values from -6 to 6
- token_tenant_index: int32 [4096], P(('groups', 'owner')), parts along dimension 0, may hold values from 0 to 31, as said below
- tenant_slot_index: int32 [64], P('groups'), parts along dimension 0, may hold values from 0 to 31, as said below
- key_matrix: bfloat16 [4096, 1024], P('owner'), may hold values from -0.09375 to 0.09375
- adapter_down_weight: bfloat16 [4096, 4096], P(None, ('groups', 'owner')), parts along dimension 1, may hold values from -0.09375 to 0.09375
- adapter_up_weight: bfloat16 [4096, 1024], P(('groups', 'owner')), parts along dimension 0, may hold values from -0.75 to 0.75
Outputs:
- input_grads: bfloat16 [4096, 4096], P(('groups', 'owner')), parts along dimension 0
- down_grads: bfloat16 [4096, 4096], P(None, ('groups', 'owner')), parts along dimension 1
- up_grads: bfloat16 [4096, 1024], P(('groups', 'owner')), parts along dimension 0
There are 2 independent parts, one for each index of `groups`. A program takes and returns all parts, laid end to end along the dimension named above; an argument that names none is the same for every part. Nothing has to cross between parts.
Inputs may be any that keep to these rules, and one draw needn't show every extreme that they name: `token_tenant_index`: the tokens of one device (aligned blocks of 128) name tenants of at most 16 tokens a holding device, where tenant k is held by device tenant_slot_index[k] // 2; in every draw one holding device gets exactly 16 tokens from every device. `tenant_slot_index`: A permutation of the slots.
All inputs are finite; a program needn't handle non-finite values.
Results may differ from a plain program's by a relative error of at most 0.0055.
Values may be sent and summed in bfloat16 or wider, within the bound.
A program may use at most 64 MiB of HBM per device.

v0:
```python
import jax
import jax.numpy as jnp
from jax import lax
from jax.sharding import PartitionSpec as P

ADAPTER_RANK = 64
TEN_DEV = 2


adapter_scale = 2.0
gradient_norm = 1.0 / 64.0


def slot_holder_products(
    received_input, received_gradient, received_tenant, adapter_down_weight, adapter_up_weight
):
    column_tenant = jnp.arange(TEN_DEV * ADAPTER_RANK, dtype=jnp.int32) // ADAPTER_RANK
    valid_mask = received_tenant[:, None] == column_tenant[None, :]
    reduced_input = jnp.where(
        valid_mask,
        jnp.dot(received_input, adapter_down_weight, preferred_element_type=jnp.float32),
        0.0,
    ).astype(jnp.bfloat16)
    backward_pass = lax.dot_general(
        received_gradient,
        adapter_up_weight,
        (((1,), (1,)), ((), ())),
        preferred_element_type=jnp.float32,
    )
    reduced_gradient = jnp.where(valid_mask, adapter_scale * backward_pass, 0.0).astype(
        jnp.bfloat16
    )
    down_grads = (
        gradient_norm
        * lax.dot_general(
            received_input,
            reduced_gradient,
            (((0,), (0,)), ((), ())),
            preferred_element_type=jnp.float32,
        )
    ).astype(jnp.bfloat16)
    up_grads = (
        adapter_scale
        * gradient_norm
        * lax.dot_general(
            reduced_input,
            received_gradient,
            (((0,), (0,)), ((), ())),
            preferred_element_type=jnp.float32,
        )
    ).astype(jnp.bfloat16)
    adapter_part = lax.dot_general(
        reduced_gradient,
        adapter_down_weight,
        (((1,), (1,)), ((), ())),
        preferred_element_type=jnp.float32,
    ).astype(jnp.bfloat16)
    return (adapter_part, down_grads, up_grads)


def frozen_product(output_gradient_rows, key_matrix):
    return lax.dot_general(
        output_gradient_rows,
        lax.all_gather(key_matrix, "owner", axis=0, tiled=True),
        (((1,), (1,)), ((), ())),
        preferred_element_type=jnp.float32,
    )


def shards(
    token_input_rows,
    output_gradient_rows,
    token_tenant_index,
    tenant_slot_index,
    key_matrix,
    adapter_down_weight,
    adapter_up_weight,
):
    holders = lax.axis_size("owner")
    row_count = token_input_rows.shape[0]
    feat_width = token_input_rows.shape[1]
    grad_width = output_gradient_rows.shape[1]
    capacity = 2 * row_count // holders
    total_slots = holders * capacity
    slot_of = tenant_slot_index[token_tenant_index]
    target = slot_of // TEN_DEV
    local_index = slot_of % TEN_DEV
    onehot = (target[:, None] == jnp.arange(holders, dtype=jnp.int32)[None, :]).astype(jnp.int32)
    earlier = jnp.cumsum(onehot, axis=0) - onehot
    bucket_place = target * capacity + jnp.sum(earlier * onehot, axis=1)
    send_x = (
        jnp.zeros((total_slots, feat_width), jnp.bfloat16)
        .at[bucket_place]
        .set(token_input_rows)
        .reshape(holders, capacity, feat_width)
    )
    send_g = (
        jnp.zeros((total_slots, grad_width), jnp.bfloat16)
        .at[bucket_place]
        .set(output_gradient_rows)
        .reshape(holders, capacity, grad_width)
    )
    send_id = (
        jnp.full((total_slots,), -1, jnp.int32)
        .at[bucket_place]
        .set(local_index)
        .reshape(holders, capacity)
    )
    received_input, received_gradient, received_tenant = (
        lax.all_to_all(send_x, "owner", split_axis=0, concat_axis=0, tiled=True),
        lax.all_to_all(send_g, "owner", split_axis=0, concat_axis=0, tiled=True),
        lax.all_to_all(send_id, "owner", split_axis=0, concat_axis=0, tiled=True),
    )
    adapter_part, down_grads, up_grads = slot_holder_products(
        received_input.reshape(total_slots, feat_width),
        received_gradient.reshape(total_slots, grad_width),
        received_tenant.reshape(total_slots),
        adapter_down_weight,
        adapter_up_weight,
    )
    returned = lax.all_to_all(
        adapter_part.reshape(holders, capacity, feat_width),
        "owner",
        split_axis=0,
        concat_axis=0,
        tiled=True,
    )
    mine = returned.reshape(total_slots, feat_width)[bucket_place]
    base = frozen_product(output_gradient_rows, key_matrix)
    input_grads = (base + mine.astype(jnp.float32)).astype(jnp.bfloat16)
    return (input_grads, down_grads, up_grads)


def solution(mesh):
    return jax.shard_map(
        shards,
        mesh=mesh,
        in_specs=(
            P(("groups", "owner"), None),
            P(("groups", "owner"), None),
            P(("groups", "owner")),
            P("groups"),
            P("owner", None),
            P(None, ("groups", "owner")),
            P(("groups", "owner"), None),
        ),
        out_specs=(
            P(("groups", "owner"), None),
            P(None, ("groups", "owner")),
            P(("groups", "owner"), None),
        ),
        check_vma=False,
    )
```

profile of v0, /device:TPU:27, one launch (start us, length us, event | category | flops | bytes accessed | tf_op | source)
XLA Modules:
  0.0 204.4 jit_solution(9168436489034516289)
XLA Ops:
  7.2 0.0 copy-start
  7.2 0.0 all-gather.2.cloned.1.call-start
  7.2 0.7 all-gather.2.cloned.1.call-update
  7.9 0.7 compare_select_fusion.1
  8.6 1.6 gather_fusion
  10.2 0.1 fusion.13
  10.3 0.2 reduce_window_sum.11
  10.4 0.2 select_reduce_fusion
  10.6 1.0 scatter_custom_fusion
  11.6 0.7 all_to_all.15
  12.3 6.3 %all-to-all-start = ((s32[16,1,16]{2,1,0:T(1,128)}), s32[16,1,16]{2,1,0:T(1,128)S(1)}, u32[]{:S(2)}, u32[]{:S(2)}) async-start(s32[16,1,16]{2,1,0:T(1,128)} %all_to_all.15), calls=%async_computation | async-start | bytes 16384 | tf_op jit(solution)/shard_map/all_to_all | solution.py:112
  18.7 2.4 %scatter_custom_fusion.1 = bf16[256,1024]{1,0:T(8,128)(2,1)} fusion(s32[128]{0:T(128)S(1)} %fusion.15, bf16[128,1024]{1,0:T(8,128)(2,1)} %param.8, bf16[]{:T(256)} %constant.58.clone.1), kind=kCustom, calls=%fused_computation.19 | custom fusion | bytes 524800 | tf_op jit(solution)/shard_map/scatter | solution.py:100
  21.0 0.0 all-to-all-done
  21.0 7.6 %all-to-all-start.1 = ((bf16[16,16,1024]{2,1,0:T(8,128)(2,1)}), bf16[16,16,1024]{2,1,0:T(8,128)(2,1)S(1)}, u32[]{:S(2)}, u32[]{:S(2)}) async-start(bf16[16,16,1024]{2,1,0:T(8,128)(2,1)} %bitcast.3), calls=%async_computation.1 | async-start | bytes 1048576 | tf_op jit(solution)/shard_map/all_to_all | solution.py:111
  28.6 4.3 %scatter_custom_fusion.2 = bf16[256,4096]{1,0:T(8,128)(2,1)} fusion(s32[128]{0:T(128)S(1)} %fusion.15, bf16[128,4096]{1,0:T(8,128)(2,1)} %param.7, bf16[]{:T(256)} %constant.58.clone.1), kind=kCustom, calls=%fused_computation.17 | custom fusion | bytes 2097664 | tf_op jit(solution)/shard_map/scatter | solution.py:94
  32.9 16.4 %all-to-all-done.1 = bf16[16,16,1024]{2,1,0:T(8,128)(2,1)S(1)} async-done(((bf16[16,16,1024]{2,1,0:T(8,128)(2,1)}), bf16[16,16,1024]{2,1,0:T(8,128)(2,1)S(1)}, u32[]{:S(2)}, u32[]{:S(2)}) %all-to-all-start.1) | async-done | bytes 524320 | tf_op jit(solution)/shard_map/all_to_all | solution.py:111
  49.3 0.8 copy-done.2
  50.1 6.1 %all-to-all-start.3 = ((bf16[16,16,4096]{2,1,0:T(8,128)(2,1)}), bf16[16,16,4096]{2,1,0:T(8,128)(2,1)S(1)}, u32[]{:S(2)}, u32[]{:S(2)}) async-start(bf16[16,16,4096]{2,1,0:T(8,128)(2,1)} %bitcast.36), calls=%async_computation.3 | async-start | bytes 4194304 | tf_op jit(solution)/shard_map/all_to_all | solution.py:110
  56.1 0.5 broadcast.164
  56.6 0.7 reduce.3
  57.3 0.1 eq.33
  57.4 0.0 copy-done.4
  57.4 1.4 fusion.5
  58.8 2.1 %convolution_convert_fusion = bf16[256,4096]{1,0:T(8,128)(2,1)} fusion(bf16[256,128]{1,0:T(8,128)(2,1)S(1)} %fusion.5, bf16[4096,128]{1,0:T(8,128)(2,1)S(1)} %copy-done), kind=kOutput, calls=%fused_computation.5 | convolution fusion | flops 269484032 | bytes 3211264 | tf_op jit(solution)/shard_map/dot_general | solution.py:52
  60.8 73.2 %all-to-all-done.3 = bf16[16,16,4096]{2,1,0:T(8,128)(2,1)S(1)} async-done(((bf16[16,16,4096]{2,1,0:T(8,128)(2,1)}), bf16[16,16,4096]{2,1,0:T(8,128)(2,1)S(1)}, u32[]{:S(2)}, u32[]{:S(2)}) %all-to-all-start.3) | async-done | bytes 2097184 | tf_op jit(solution)/shard_map/all_to_all | solution.py:110
  134.1 1.3 copy-done.1
  135.4 6.1 %all-to-all-start.2 = ((bf16[16,16,4096]{2,1,0:T(8,128)(2,1)}), bf16[16,16,4096]{2,1,0:T(8,128)(2,1)S(1)}, u32[]{:S(2)}, u32[]{:S(2)}) async-start(bf16[16,16,4096]{2,1,0:T(8,128)(2,1)} %bitcast.37), calls=%async_computation.2 | async-start | bytes 4194304 | tf_op jit(solution)/shard_map/all_to_all | solution.py:121
  141.5 3.3 %fusion.1 = bf16[4096,128]{1,0:T(8,128)(2,1)} fusion(bf16[256,4096]{1,0:T(8,128)(2,1)} %bitcast.34, bf16[256,128]{1,0:T(8,128)(2,1)S(1)} %fusion.5), kind=kOutput, calls=%fused_computation.9 | convolution fusion | flops 269484032 | bytes 3211264 | tf_op jit(solution)/shard_map/dot_general | solution.py:35
  144.8 3.3 %fusion.2 = bf16[128,1024]{1,0:T(8,128)(2,1)} fusion(bf16[256,1024]{1,0:T(8,128)(2,1)} %bitcast.39, bf16[256,4096]{1,0:T(8,128)(2,1)} %bitcast.35, bf16[4096,128]{1,0:T(8,128)(2,1)S(1)} %copy-done, s32[128]{0:T(128)S(1)} %and_select_fusion, s32[256]{0:T(256)S(1)} %eq.33), kind=kOutput, calls=%fused_computation.11 | convolution fusion | flops 335904768 | bytes 3933696 | tf_op jit(solution)/shard_map/dot_general | solution.py:45
  148.1 39.8 %all-to-all-done.2 = bf16[16,16,4096]{2,1,0:T(8,128)(2,1)S(1)} async-done(((bf16[16,16,4096]{2,1,0:T(8,128)(2,1)}), bf16[16,16,4096]{2,1,0:T(8,128)(2,1)S(1)}, u32[]{:S(2)}, u32[]{:S(2)}) %all-to-all-start.2) | async-done | bytes 2097184 | tf_op jit(solution)/shard_map/all_to_all | solution.py:121
  187.9 2.2 %gather_fusion.1 = bf16[128,4096]{1,0:T(8,128)(2,1)} fusion(bf16[256,4096]{1,0:T(8,128)(2,1)S(1)} %bitcast.33, s32[1024]{0:T(1024)S(1)} %pad_clamp_fusion), kind=kCustom, calls=%fused_computation.1 | custom fusion | bytes 2097664 | tf_op jit(solution)/shard_map/gather | solution.py:128
  190.1 7.5 %fusion = bf16[128,4096]{1,0:T(8,128)(2,1)} fusion(bf16[128,1024]{1,0:T(8,128)(2,1)S(1)} %copy-done.3, bf16[4096,1024]{1,0:T(8,128)(2,1)} %all-gather.2.cloned.1.call-done, bf16[128,4096]{1,0:T(8,128)(2,1)} %gather_fusion.1), kind=kOutput, calls=%fused_computation.8 | convolution fusion | flops 1075314688 | bytes 10747904 | tf_op jit(solution)/shard_map/dot_general | solution.py:62
  (12 shorter events, 0.1 us)
Async XLA Ops:
  7.2 51.6 %copy-start = (bf16[4096,128]{1,0:T(8,128)(2,1)S(1)}, bf16[4096,128]{1,0:T(8,128)(2,1)}, u32[]{:S(2)}) copy-start(bf16[4096,128]{1,0:T(8,128)(2,1)} %param.12) | copy-start | bytes 3145732
  7.2 182.9 %all-gather.2.cloned.1.call-start = ((), (), s32[]{:S(2)}) async-start(), calls=%async_computation.4 | async-start | bytes 8912896 | tf_op jit(solution)/shard_map/all_gather | solution.py:64
  12.3 8.7 %all-to-all-start = ((s32[16,1,16]{2,1,0:T(1,128)}), s32[16,1,16]{2,1,0:T(1,128)S(1)}, u32[]{:S(2)}, u32[]{:S(2)}) async-start(s32[16,1,16]{2,1,0:T(1,128)} %all_to_all.15), calls=%async_computation | async-start | bytes 16384 | tf_op jit(solution)/shard_map/all_to_all | solution.py:112
  21.0 28.2 %all-to-all-start.1 = ((bf16[16,16,1024]{2,1,0:T(8,128)(2,1)}), bf16[16,16,1024]{2,1,0:T(8,128)(2,1)S(1)}, u32[]{:S(2)}, u32[]{:S(2)}) async-start(bf16[16,16,1024]{2,1,0:T(8,128)(2,1)} %bitcast.3), calls=%async_computation.1 | async-start | bytes 1048576 | tf_op jit(solution)/shard_map/all_to_all | solution.py:111
  49.3 0.8 copy-start.2
  49.3 8.1 %copy-start.4 = (bf16[128,1024]{1,0:T(8,128)(2,1)S(1)}, bf16[128,1024]{1,0:T(8,128)(2,1)}, u32[]{:S(2)}) copy-start(bf16[128,1024]{1,0:T(8,128)(2,1)} %param.13) | copy-start | bytes 786436
  50.1 84.0 %all-to-all-start.3 = ((bf16[16,16,4096]{2,1,0:T(8,128)(2,1)}), bf16[16,16,4096]{2,1,0:T(8,128)(2,1)S(1)}, u32[]{:S(2)}, u32[]{:S(2)}) async-start(bf16[16,16,4096]{2,1,0:T(8,128)(2,1)} %bitcast.36), calls=%async_computation.3 | async-start | bytes 4194304 | tf_op jit(solution)/shard_map/all_to_all | solution.py:110
  134.1 1.3 copy-start.1
  135.4 52.5 %all-to-all-start.2 = ((bf16[16,16,4096]{2,1,0:T(8,128)(2,1)}), bf16[16,16,4096]{2,1,0:T(8,128)(2,1)S(1)}, u32[]{:S(2)}, u32[]{:S(2)}) async-start(bf16[16,16,4096]{2,1,0:T(8,128)(2,1)} %bitcast.37), calls=%async_computation.2 | async-start | bytes 4194304 | tf_op jit(solution)/shard_map/all_to_all | solution.py:121
  187.9 2.2 %copy-start.3 = (bf16[128,1024]{1,0:T(8,128)(2,1)S(1)}, bf16[128,1024]{1,0:T(8,128)(2,1)}, u32[]{:S(2)}) copy-start(bf16[128,1024]{1,0:T(8,128)(2,1)} %param.8) | copy-start | bytes 786436
Sparse Core Ops, SparseCore 0:
  10.2 120.1 all-gather.1
where the time goes:
time: 206 us; the launch traced here: 204 us
  waiting for transfers between devices  130 us (63%)
  starting transfers between devices  26 us (13%)
  matrix products  17.6 us (9%)
  local copies, waits for them, and re-layouts  14.8 us (7%)
  between operations  14.1 us (7%)
    all_to_all x1, waiting for transfers between devices, shards(): lax.all_to_all(send_x, 'owner', split_axis=0, concat_axis=0, tiled=True)  73.2 us
    all_to_all x1, waiting for transfers between devices, shards(): lax.all_to_all(adapter_part.reshape(holders, capacity, feat_width), 'owne...  39.8 us
    all_to_all x1, waiting for transfers between devices, shards(): lax.all_to_all(send_g, 'owner', split_axis=0, concat_axis=0, tiled=True)  16.4 us
    all_to_all x1, starting transfers between devices, shards(): lax.all_to_all(send_g, 'owner', split_axis=0, concat_axis=0, tiled=True)  7.58 us
    dot_general x1, matrix products, frozen_product(): lax.dot_general(output_gradient_rows, lax.all_gather(key_matrix, 'owner',...  7.47 us
    all_to_all x1, starting transfers between devices, shards(): lax.all_to_all(send_id, 'owner', split_axis=0, concat_axis=0, tiled=True)  6.33 us
    all_to_all x1, starting transfers between devices, shards(): lax.all_to_all(send_x, 'owner', split_axis=0, concat_axis=0, tiled=True)  6.05 us
    all_to_all x1, starting transfers between devices, shards(): lax.all_to_all(adapter_part.reshape(holders, capacity, feat_width), 'owne...  6.05 us
  transfers between devices with their start and end apart: 5, of which 3 were waited for; matrix products, arithmetic and copies ran while one was open for 12% of the time, Pallas kernels for 0%

commit v1 on v0

--- a/solution.py
+++ b/solution.py
@@ -1,6 +1,10 @@
+import functools
+
 import jax
 import jax.numpy as jnp
 from jax import lax
+from jax.experimental import pallas as pl
+from jax.experimental.pallas import tpu as pltpu
 from jax.sharding import PartitionSpec as P
 
 ADAPTER_RANK = 64
@@ -64,6 +68,325 @@
         lax.all_gather(key_matrix, "owner", axis=0, tiled=True),
         (((1,), (1,)), ((), ())),
         preferred_element_type=jnp.float32,
+    )
+
+
+MESH = pl.DeviceIdType.MESH
+NT = (((1,), (1,)), ((), ()))
+TN = (((0,), (0,)), ((), ()))
+COLUMNS = 512
+RING = 8
+
+
+def matmul(a, b, dims=(((1,), (0,)), ((), ()))):
+    return lax.dot_general(a, b, dims, preferred_element_type=jnp.float32)
+
+
+def ring_chip(position):
+    up = (position < 4).astype(jnp.int32)
+    z = up * position + (1 - up) * (7 - position)
+    return z * 2 + (1 - up)
+
+
+def fused_kernel(
+    n,
+    cap,
+    place_ref,
+    place_t_ref,
+    local_ref,
+    x_ref,
+    g_ref,
+    k_ref,
+    down_ref,
+    up_ref,
+    out_ref,
+    down_grads_ref,
+    up_grads_ref,
+    x_send,
+    x_recv,
+    g_send,
+    g_recv,
+    part,
+    returned,
+    key,
+    base,
+    reduced,
+    h_sum,
+    gs_sem,
+    gr_sem,
+    xs_sem,
+    xr_sem,
+    ps_sem,
+    pr_sem,
+    ks_sem,
+    kr_sem,
+):
+    group = lax.axis_index("groups")
+    me = lax.axis_index("owner")
+    width = x_ref.shape[1]
+    grad = g_ref.shape[1]
+    tiles = width // COLUMNS
+    core = me % 2
+    chip = me // 2
+    z, x = chip // 2, chip % 2
+    position = (1 - x) * z + x * (7 - z)
+    step_by = 1 - 2 * core
+    sibling = (group, chip * 2 + 1 - core)
+    across = (1 - group, me)
+    ahead = (group, ring_chip((position + step_by + RING) % RING) * 2 + core)
+
+    barrier = pltpu.get_barrier_semaphore()
+
+    @pl.loop(1, n)
+    def _(i):
+        pl.semaphore_signal(barrier, inc=1, device_id=(group, (me + i) % n), device_id_type=MESH)
+
+    pl.semaphore_signal(barrier, inc=1, device_id=across, device_id_type=MESH)
+
+    def rows_of(owner):
+        return pl.ds(pl.multiple_of(owner * cap, cap), cap)
+
+    def row_copy(src, dst, send, recv, at, owner, i):
+        return pltpu.make_async_remote_copy(
+            src_ref=src.at[rows_of(owner)],
+            dst_ref=dst.at[rows_of(at)],
+            send_sem=send.at[i],
+            recv_sem=recv.at[i],
+            device_id=(group, owner),
+            device_id_type=MESH,
+        )
+
+    def start_all(src, dst, send, recv):
+        @pl.loop(1, n)
+        def _(i):
+            row_copy(src, dst, send, recv, me, (me + i) % n, i).start()
+
+    def wait_arrivals(src, dst, send, recv):
+        @pl.loop(1, n)
+        def _(i):
+            row_copy(src, dst, send, recv, (me + n - i) % n, (me + i) % n, i).wait_recv()
+
+    def wait_sent(src, dst, send, recv):
+        @pl.loop(1, n)
+        def _(i):
+            row_copy(src, dst, send, recv, me, (me + i) % n, i).wait_send()
+
+    half = k_ref.shape[0] // 2
+
+    def key_rows(at_position, of_core, of_half):
+        owner = ring_chip(at_position) * 2 + of_core
+        return pl.ds(pl.multiple_of((owner * 2 + of_half) * half, half), half)
+
+    def key_copy(rows, sem, device, src=None):
+        return pltpu.make_async_remote_copy(
+            src_ref=key.at[rows] if src is None else src,
+            dst_ref=key.at[rows],
+            send_sem=ks_sem.at[sem],
+            recv_sem=kr_sem.at[sem],
+            device_id=device,
+            device_id_type=MESH,
+        )
+
+    def origin(s):
+        return (position + (RING - s) * step_by + 2 * RING * RING) % RING
+
+    def sibling_origin(s):
+        return (position - (RING - s) * step_by + 2 * RING * RING) % RING
+
+    def ring_copy(s):
+        if s == 0:
+            return key_copy(
+                key_rows(position, core, group),
+                0,
+                ahead,
+                k_ref.at[pl.ds(pl.multiple_of(group * half, half), half)],
+            )
+        return key_copy(key_rows(origin(s), core, group), s, ahead)
+
+    def ring_arrival(s):
+        return key_copy(key_rows(origin(s + 1), core, group), s, ahead)
+
+    def across_copy(s):
+        return key_copy(key_rows(origin(s + 1), core, group), 7 + s, across)
+
+    def across_arrival(s):
+        return key_copy(key_rows(origin(s + 1), core, 1 - group), 7 + s, across)
+
+    def sibling_copy(s, far):
+        return key_copy(
+            key_rows(origin(s + 1), core, 1 - group if far else group), (21 if far else 14) + s, sibling
+        )
+
+    def sibling_arrival(s, far):
+        return key_copy(
+            key_rows(sibling_origin(s + 1), 1 - core, 1 - group if far else group),
+            (21 if far else 14) + s,
+            sibling,
+        )
+
+    def own_copy(owner):
+        return pltpu.make_async_remote_copy(
+            src_ref=k_ref,
+            dst_ref=key.at[pl.ds(pl.multiple_of(owner * 2 * half, 2 * half), 2 * half)],
+            send_sem=ks_sem.at[28],
+            recv_sem=kr_sem.at[28],
+            device_id=sibling,
+            device_id_type=MESH,
+        )
+
+    g_send[:, :grad] = matmul(place_t_ref[...], g_ref[...]).astype(jnp.bfloat16)
+    g_send[:, grad:] = matmul(place_t_ref[...], local_ref[...]).astype(jnp.bfloat16)
+    pl.semaphore_wait(barrier, n)
+
+    start_all(g_send, g_recv, gs_sem, gr_sem)
+    ring_copy(0).start()
+    own_copy(me).start()
+    g_recv[rows_of(me), :] = g_send[rows_of(me), :]
+
+    @pl.loop(0, tiles)
+    def _(t):
+        at = pl.ds(pl.multiple_of(t * COLUMNS, COLUMNS), COLUMNS)
+        x_send[:, at] = matmul(place_t_ref[...], x_ref[:, at]).astype(jnp.bfloat16)
+
+    start_all(x_send, x_recv, xs_sem, xr_sem)
+    key[pl.ds(pl.multiple_of(me * 2 * half, 2 * half), 2 * half), :] = k_ref[...]
+    x_recv[rows_of(me), :] = x_send[rows_of(me), :]
+
+    wait_arrivals(g_send, g_recv, gs_sem, gr_sem)
+    mask = g_recv[:, grad:].astype(jnp.float32) > 0.5
+    reduced[...] = jnp.where(
+        mask, adapter_scale * matmul(g_recv[:, :grad], up_ref[...], NT), 0.0
+    ).astype(jnp.bfloat16)
+
+    @pl.loop(0, tiles)
+    def _(t):
+        at = pl.ds(pl.multiple_of(t * COLUMNS, COLUMNS), COLUMNS)
+        part[:, at] = matmul(reduced[...], down_ref[at, :], NT).astype(jnp.bfloat16)
+
+    start_all(part, returned, ps_sem, pr_sem)
+    returned[rows_of(me), :] = part[rows_of(me), :]
+
+    steps = RING - 1
+    for s in range(steps):
+        ring_arrival(s).wait_recv()
+        if s + 1 < steps:
+            ring_copy(s + 1).start()
+        across_copy(s).start()
+        sibling_copy(s, False).start()
+        if s:
+            across_arrival(s - 1).wait_recv()
+            sibling_copy(s - 1, True).start()
+
+    wait_arrivals(x_send, x_recv, xs_sem, xr_sem)
+    h_sum[...] = jnp.zeros_like(h_sum)
+
+    @pl.loop(0, tiles)
+    def _(t):
+        at = pl.ds(pl.multiple_of(t * COLUMNS, COLUMNS), COLUMNS)
+        h_sum[...] += matmul(x_recv[:, at], down_ref[at, :])
+        down_grads_ref[at, :] = (gradient_norm * matmul(x_recv[:, at], reduced[...], TN)).astype(
+            jnp.bfloat16
+        )
+
+    h = jnp.where(mask, h_sum[...], 0.0).astype(jnp.bfloat16)
+    up_grads_ref[...] = (adapter_scale * gradient_norm * matmul(h, g_recv[:, :grad], TN)).astype(
+        jnp.bfloat16
+    )
+
+    across_arrival(steps - 1).wait_recv()
+    sibling_copy(steps - 1, True).start()
+    own_copy(chip * 2 + 1 - core).wait_recv()
+    for s in range(steps):
+        sibling_arrival(s, False).wait_recv()
+        sibling_arrival(s, True).wait_recv()
+
+    @pl.loop(0, tiles)
+    def _(t):
+        at = pl.ds(pl.multiple_of(t * COLUMNS, COLUMNS), COLUMNS)
+        base[:, at] = matmul(g_ref[...], key[at, :], NT)
+
+    wait_arrivals(part, returned, ps_sem, pr_sem)
+
+    @pl.loop(0, tiles)
+    def _(t):
+        at = pl.ds(pl.multiple_of(t * COLUMNS, COLUMNS), COLUMNS)
+        out_ref[:, at] = (base[:, at] + matmul(place_ref[...], returned[:, at])).astype(jnp.bfloat16)
+
+    wait_sent(g_send, g_recv, gs_sem, gr_sem)
+    wait_sent(x_send, x_recv, xs_sem, xr_sem)
+    wait_sent(part, returned, ps_sem, pr_sem)
+    own_copy(me).wait_send()
+    for s in range(steps):
+        ring_copy(s).wait_send()
+        across_copy(s).wait_send()
+        sibling_copy(s, False).wait_send()
+        sibling_copy(s, True).wait_send()
+
+
+def fused_shards(
+    token_input_rows,
+    output_gradient_rows,
+    token_tenant_index,
+    tenant_slot_index,
+    key_matrix,
+    adapter_down_weight,
+    adapter_up_weight,
+):
+    holders = lax.axis_size("owner")
+    rows, width = token_input_rows.shape
+    grad = output_gradient_rows.shape[1]
+    cap = 2 * rows // holders
+    total = holders * cap
+    held = TEN_DEV * ADAPTER_RANK
+    tenants = tenant_slot_index.shape[0]
+    named = token_tenant_index[:, None] == jnp.arange(tenants, dtype=jnp.int32)[None, :]
+    slot_of = jnp.sum(jnp.where(named, tenant_slot_index[None, :], 0), axis=1)
+    target = slot_of // TEN_DEV
+    same = target[:, None] == target[None, :]
+    before = jnp.arange(rows)[None, :] < jnp.arange(rows)[:, None]
+    bucket_place = target * cap + jnp.sum((same & before).astype(jnp.int32), axis=1)
+    slots = jnp.arange(total, dtype=jnp.int32)
+    place = (bucket_place[:, None] == slots[None, :]).astype(jnp.bfloat16)
+    place_t = (bucket_place[None, :] == slots[:, None]).astype(jnp.bfloat16)
+    column = jnp.arange(held, dtype=jnp.int32) // ADAPTER_RANK
+    local = ((slot_of % TEN_DEV)[:, None] == column[None, :]).astype(jnp.bfloat16)
+    vmem = pl.BlockSpec(memory_space=pltpu.VMEM)
+    return pl.pallas_call(
+        functools.partial(fused_kernel, holders, cap),
+        out_shape=(
+            jax.ShapeDtypeStruct((rows, width), jnp.bfloat16),
+            jax.ShapeDtypeStruct((width, held), jnp.bfloat16),
+            jax.ShapeDtypeStruct((held, grad), jnp.bfloat16),
+        ),
+        in_specs=[vmem] * 8,
+        out_specs=(vmem,) * 3,
+        scratch_shapes=[
+            pltpu.VMEM((total, width), jnp.bfloat16),
+            pltpu.VMEM((total, width), jnp.bfloat16),
+            pltpu.VMEM((total, grad + held), jnp.bfloat16),
+            pltpu.VMEM((total, grad + held), jnp.bfloat16),
+            pltpu.VMEM((total, width), jnp.bfloat16),
+            pltpu.VMEM((total, width), jnp.bfloat16),
+            pltpu.VMEM((width, grad), jnp.bfloat16),
+            pltpu.VMEM((rows, width), jnp.float32),
+            pltpu.VMEM((total, held), jnp.bfloat16),
+            pltpu.VMEM((total, held), jnp.float32),
+        ]
+        + [pltpu.SemaphoreType.DMA((holders,))] * 6
+        + [pltpu.SemaphoreType.DMA((29,))] * 2,
+        compiler_params=pltpu.CompilerParams(
+            collective_id=0, has_side_effects=True, vmem_limit_bytes=48 * 2**20
+        ),
+        name="fused_backward",
+    )(
+        place,
+        place_t,
+        local,
+        token_input_rows,
+        output_gradient_rows,
+        key_matrix,
+        adapter_down_weight,
+        adapter_up_weight,
     )
 
 
@@ -132,8 +455,9 @@
 
 
 def solution(mesh):
+    on_grid = mesh.shape["groups"] == 2 and mesh.shape["owner"] == 2 * RING
     return jax.shard_map(
-        shards,
+        fused_shards if on_grid else shards,
         mesh=mesh,
         in_specs=(
             P(("groups", "owner"), None),

time: 206 us -> 166 us (0.81)
  Pallas kernels: 0 us -> 153 us
  waiting for transfers between devices: 130 us -> 0 us
  starting transfers between devices: 26 us -> 0 us
  matrix products: 17.6 us -> 0 us
  between operations: 14.1 us -> 0.69 us
  local copies, waits for them, and re-layouts: 14.8 us -> 8.03 us
    pallas_call x0 -> x1, Pallas kernels: none -> 153 us  [fused_shards(): pl.pallas_call(functools.partial(fused_kernel, holders, cap), out_shape=(...]
    all_to_all x4 -> x0, waiting for transfers between devices: 129 us -> none  [the longest x1 73.2 us: shards(): lax.all_to_all(send_x, 'owner', split_axis=0, concat_axis=0, tiled=True)]
    all_to_all x4 -> x0, starting transfers between devices: 26 us -> none  [the longest x1 7.58 us: shards(): lax.all_to_all(send_g, 'owner', split_axis=0, concat_axis=0, tiled=True)]
    dot_general x5 -> x0, matrix products: 17.6 us -> none  [the longest x1 7.47 us: frozen_product(): lax.dot_general(output_gradient_rows, lax.all_gather(key_matrix, 'owner',...]
    scatter x3 -> x0, local copies, waits for them, and re-layouts: 7.66 us -> none  [the longest x1 4.3 us: shards(): send_x = jnp.zeros((total_slots, feat_width), jnp.bfloat16).at[bucket_pla...]
    unnamed x10 -> x13, local copies, waits for them, and re-layouts: 2.11 us -> 8.03 us
    gather x2 -> x0, local copies, waits for them, and re-layouts: 3.74 us -> none  [the longest x1 2.16 us: shards(): mine = returned.reshape(total_slots, feat_width)[bucket_place]]
  transfers between devices with their start and end apart: 5 -> 0, of which waited for: 3 -> 0; matrix products, arithmetic and copies ran while one was open for 12% -> 0% of each run, Pallas kernels for 0% -> 0%
where the time goes in v1:
time: 166 us; the launch traced here: 163 us
  Pallas kernels  153 us (92%)
  local copies, waits for them, and re-layouts  8.03 us (5%)
    pallas_call x1, Pallas kernels, fused_shards(): pl.pallas_call(functools.partial(fused_kernel, holders, cap), out_shape=(...  153 us
    unnamed x13, local copies, waits for them, and re-layouts  8.03 us

profile of v1, /device:TPU:27, one launch (start us, length us, event | category | flops | bytes accessed | tf_op | source)
XLA Modules:
  0.0 162.8 jit_solution(3414399794630019275)
XLA Ops:
  0.6 0.8 select_reduce_fusion
  1.4 0.2 convert_reduce_fusion
  1.6 0.1 compare_convert_fusion.local_ref
  1.7 0.1 fusion.place_ref
  1.8 0.0 copy-start
  1.8 1.2 copy-done
  3.0 0.0 copy-start.1
  3.0 1.2 copy-done.1
  4.3 0.0 copy-start.2
  4.3 1.0 copy-done.2
  5.3 0.0 copy-start.3
  5.3 0.9 copy-done.3
  6.3 0.0 copy-start.4
  6.3 0.9 copy-done.4
  7.2 153.0 %fused_backward.1 = (bf16[128,4096]{1,0:T(8,128)(2,1)S(1)}, bf16[4096,128]{1,0:T(8,128)(2,1)S(1)}, bf16[128,1024]{1,0:T(8,128)(2,1)S(1)}) custom-call(bf16[128,256]{1,0:T(8,128)(2,1)S(1)} %fusion.place_ref, bf16[256,128]{1,0:T(8,128)(2,1)S(1)} %fusion.1.place_t_ref, bf16[128,128]{1,0:T(8,128)(2,1)S(1)} %compare_convert_fusion.local_ref, ...), custom_call_target="tpu_custom_call" | custom-call | tf_op jit(solution)/shard_map/fused_backward/pallas_call | solution.py:354
  160.2 1.0 copy.13
  161.2 1.0 copy.14
  162.1 0.7 copy.15
  (3 shorter events, 0.0 us)
Async XLA Ops:
  1.8 1.2 copy-start
  3.0 1.2 copy-start.1
  4.3 1.0 copy-start.2
  5.3 0.9 copy-start.3
  6.3 0.9 copy-start.4

commit v2 on v1

--- a/solution.py
+++ b/solution.py
@@ -75,6 +75,8 @@
 NT = (((1,), (1,)), ((), ()))
 TN = (((0,), (0,)), ((), ()))
 COLUMNS = 512
+AHEAD = 2
+EACH = 2
 RING = 8
 
 
@@ -94,11 +96,11 @@
     place_ref,
     place_t_ref,
     local_ref,
-    x_ref,
-    g_ref,
-    k_ref,
-    down_ref,
-    up_ref,
+    x_hbm,
+    g_hbm,
+    k_hbm,
+    down_hbm,
+    up_hbm,
     out_ref,
     down_grads_ref,
     up_grads_ref,
@@ -112,6 +114,12 @@
     base,
     reduced,
     h_sum,
+    x_ref,
+    g_ref,
+    k_ref,
+    down_ref,
+    up_ref,
+    in_sem,
     gs_sem,
     gr_sem,
     xs_sem,
@@ -135,6 +143,21 @@
     across = (1 - group, me)
     ahead = (group, ring_chip((position + step_by + RING) % RING) * 2 + core)
 
+    loads = [
+        pltpu.make_async_copy(src, dst, in_sem.at[i])
+        for i, (src, dst) in enumerate(
+            [
+                (g_hbm, g_ref),
+                (k_hbm, k_ref),
+                (x_hbm, x_ref),
+                (up_hbm, up_ref),
+                (down_hbm, down_ref),
+            ]
+        )
+    ]
+    for load in loads:
+        load.start()
+
     barrier = pltpu.get_barrier_semaphore()
 
     @pl.loop(1, n)
@@ -234,36 +257,49 @@
             device_id_type=MESH,
         )
 
+    loads[0].wait()
     g_send[:, :grad] = matmul(place_t_ref[...], g_ref[...]).astype(jnp.bfloat16)
     g_send[:, grad:] = matmul(place_t_ref[...], local_ref[...]).astype(jnp.bfloat16)
     pl.semaphore_wait(barrier, n)
 
     start_all(g_send, g_recv, gs_sem, gr_sem)
+    loads[1].wait()
     ring_copy(0).start()
     own_copy(me).start()
     g_recv[rows_of(me), :] = g_send[rows_of(me), :]
+    loads[2].wait()
 
     @pl.loop(0, tiles)
     def _(t):
         at = pl.ds(pl.multiple_of(t * COLUMNS, COLUMNS), COLUMNS)
         x_send[:, at] = matmul(place_t_ref[...], x_ref[:, at]).astype(jnp.bfloat16)
 
-    start_all(x_send, x_recv, xs_sem, xr_sem)
+    x_queue = [(x_send, x_recv, xs_sem, xr_sem, i) for i in range(1, n)]
+    part_queue = [(part, returned, ps_sem, pr_sem, i) for i in range(1, n)]
+    queue = x_queue + part_queue
+
+    def start_some(count):
+        for _ in range(min(count, len(queue))):
+            src, dst, send, recv, i = queue.pop(0)
+            row_copy(src, dst, send, recv, me, (me + i) % n, i).start()
+
+    start_some(AHEAD)
     key[pl.ds(pl.multiple_of(me * 2 * half, 2 * half), 2 * half), :] = k_ref[...]
     x_recv[rows_of(me), :] = x_send[rows_of(me), :]
 
     wait_arrivals(g_send, g_recv, gs_sem, gr_sem)
+    loads[3].wait()
     mask = g_recv[:, grad:].astype(jnp.float32) > 0.5
     reduced[...] = jnp.where(
         mask, adapter_scale * matmul(g_recv[:, :grad], up_ref[...], NT), 0.0
     ).astype(jnp.bfloat16)
+    loads[4].wait()
 
     @pl.loop(0, tiles)
     def _(t):
         at = pl.ds(pl.multiple_of(t * COLUMNS, COLUMNS), COLUMNS)
         part[:, at] = matmul(reduced[...], down_ref[at, :], NT).astype(jnp.bfloat16)
 
-    start_all(part, returned, ps_sem, pr_sem)
     returned[rows_of(me), :] = part[rows_of(me), :]
 
     steps = RING - 1
@@ -276,6 +312,8 @@
         if s:
             across_arrival(s - 1).wait_recv()
             sibling_copy(s - 1, True).start()
+        start_some(EACH)
+    start_some(2 * n)
 
     wait_arrivals(x_send, x_recv, xs_sem, xr_sem)
     h_sum[...] = jnp.zeros_like(h_sum)
@@ -358,7 +396,7 @@
             jax.ShapeDtypeStruct((width, held), jnp.bfloat16),
             jax.ShapeDtypeStruct((held, grad), jnp.bfloat16),
         ),
-        in_specs=[vmem] * 8,
+        in_specs=[vmem] * 3 + [pl.BlockSpec(memory_space=pl.ANY)] * 5,
         out_specs=(vmem,) * 3,
         scratch_shapes=[
             pltpu.VMEM((total, width), jnp.bfloat16),
@@ -371,6 +409,12 @@
             pltpu.VMEM((rows, width), jnp.float32),
             pltpu.VMEM((total, held), jnp.bfloat16),
             pltpu.VMEM((total, held), jnp.float32),
+            pltpu.VMEM((rows, width), jnp.bfloat16),
+            pltpu.VMEM((rows, grad), jnp.bfloat16),
+            pltpu.VMEM(key_matrix.shape, jnp.bfloat16),
+            pltpu.VMEM((width, held), jnp.bfloat16),
+            pltpu.VMEM((held, grad), jnp.bfloat16),
+            pltpu.SemaphoreType.DMA((5,)),
         ]
         + [pltpu.SemaphoreType.DMA((holders,))] * 6
         + [pltpu.SemaphoreType.DMA((29,))] * 2,

time: 166 us -> 148 us (0.89); the launches traced: 163 us -> 148 us
  Pallas kernels: 153 us -> 138 us
    pallas_call x1, Pallas kernels: 153 us -> 138 us  [fused_shards(): pl.pallas_call(functools.partial(fused_kernel, holders, cap), out_shape=(...]
where the time goes in v2:
time: 148 us
  Pallas kernels  138 us (93%)
  local copies, waits for them, and re-layouts  8.03 us (5%)
    pallas_call x1, Pallas kernels, fused_shards(): pl.pallas_call(functools.partial(fused_kernel, holders, cap), out_shape=(...  138 us
    unnamed x13, local copies, waits for them, and re-layouts  8.03 us

profile of v2, /device:TPU:27, one launch (start us, length us, event | category | flops | bytes accessed | tf_op | source)
XLA Modules:
  0.0 147.7 jit_solution(9510521749012229126)
XLA Ops:
  0.6 0.8 select_reduce_fusion
  1.4 0.2 convert_reduce_fusion
  1.6 0.1 compare_convert_fusion.local_ref
  1.7 0.1 fusion.place_ref
  1.8 0.0 copy-start
  1.8 1.2 copy-done
  3.0 0.0 copy-start.1
  3.0 1.2 copy-done.1
  4.3 0.0 copy-start.2
  4.3 1.0 copy-done.2
  5.3 0.0 copy-start.3
  5.3 0.9 copy-done.3
  6.3 0.0 copy-start.4
  6.3 0.9 copy-done.4
  7.2 137.8 %fused_backward.1 = (bf16[128,4096]{1,0:T(8,128)(2,1)S(1)}, bf16[4096,128]{1,0:T(8,128)(2,1)S(1)}, bf16[128,1024]{1,0:T(8,128)(2,1)S(1)}) custom-call(bf16[128,256]{1,0:T(8,128)(2,1)S(1)} %fusion.place_ref, bf16[256,128]{1,0:T(8,128)(2,1)S(1)} %fusion.1.place_t_ref, bf16[128,128]{1,0:T(8,128)(2,1)S(1)} %compare_convert_fusion.local_ref, ...), custom_call_target="tpu_custom_call" | custom-call | tf_op jit(solution)/shard_map/fused_backward/pallas_call | solution.py:392
  145.0 1.0 copy.13
  146.0 1.0 copy.14
  147.0 0.7 copy.15
  (3 shorter events, 0.0 us)
Async XLA Ops:
  1.8 1.2 copy-start
  3.0 1.2 copy-start.1
  4.3 1.0 copy-start.2
  5.3 0.9 copy-start.3
  6.3 0.9 copy-start.4

commit v3 on v2

--- a/solution.py
+++ b/solution.py
@@ -75,19 +75,13 @@
 NT = (((1,), (1,)), ((), ()))
 TN = (((0,), (0,)), ((), ()))
 COLUMNS = 512
-AHEAD = 2
+AHEAD = 8
 EACH = 2
-RING = 8
+LAYERS = 4
 
 
 def matmul(a, b, dims=(((1,), (0,)), ((), ()))):
     return lax.dot_general(a, b, dims, preferred_element_type=jnp.float32)
-
-
-def ring_chip(position):
-    up = (position < 4).astype(jnp.int32)
-    z = up * position + (1 - up) * (7 - position)
-    return z * 2 + (1 - up)
 
 
 def fused_kernel(
@@ -137,11 +131,9 @@
     core = me % 2
     chip = me // 2
     z, x = chip // 2, chip % 2
-    position = (1 - x) * z + x * (7 - z)
-    step_by = 1 - 2 * core
     sibling = (group, chip * 2 + 1 - core)
     across = (1 - group, me)
-    ahead = (group, ring_chip((position + step_by + RING) % RING) * 2 + core)
+    beside = (group, (z * 2 + 1 - x) * 2 + core)
 
     loads = [
         pltpu.make_async_copy(src, dst, in_sem.at[i])
@@ -196,63 +188,68 @@
 
     half = k_ref.shape[0] // 2
 
-    def key_rows(at_position, of_core, of_half):
-        owner = ring_chip(at_position) * 2 + of_core
+    def key_rows(of_z, of_x, of_core, of_half):
+        owner = (of_z * 2 + of_x) * 2 + of_core
         return pl.ds(pl.multiple_of((owner * 2 + of_half) * half, half), half)
 
-    def key_copy(rows, sem, device, src=None):
+    def key_copy(rows, sent, landed, device, own=False):
+        src = k_ref.at[pl.ds(pl.multiple_of(group * half, half), half)] if own else key.at[rows]
         return pltpu.make_async_remote_copy(
-            src_ref=key.at[rows] if src is None else src,
+            src_ref=src,
             dst_ref=key.at[rows],
-            send_sem=ks_sem.at[sem],
-            recv_sem=kr_sem.at[sem],
+            send_sem=ks_sem.at[sent],
+            recv_sem=kr_sem.at[landed],
             device_id=device,
             device_id_type=MESH,
         )
 
-    def origin(s):
-        return (position + (RING - s) * step_by + 2 * RING * RING) % RING
-
-    def sibling_origin(s):
-        return (position - (RING - s) * step_by + 2 * RING * RING) % RING
-
-    def ring_copy(s):
-        if s == 0:
-            return key_copy(
-                key_rows(position, core, group),
-                0,
-                ahead,
-                k_ref.at[pl.ds(pl.multiple_of(group * half, half), half)],
-            )
-        return key_copy(key_rows(origin(s), core, group), s, ahead)
-
-    def ring_arrival(s):
-        return key_copy(key_rows(origin(s + 1), core, group), s, ahead)
-
-    def across_copy(s):
-        return key_copy(key_rows(origin(s + 1), core, group), 7 + s, across)
-
-    def across_arrival(s):
-        return key_copy(key_rows(origin(s + 1), core, 1 - group), 7 + s, across)
-
-    def sibling_copy(s, far):
-        return key_copy(
-            key_rows(origin(s + 1), core, 1 - group if far else group), (21 if far else 14) + s, sibling
-        )
-
-    def sibling_arrival(s, far):
-        return key_copy(
-            key_rows(sibling_origin(s + 1), 1 - core, 1 - group if far else group),
-            (21 if far else 14) + s,
-            sibling,
-        )
+    def z_copy(of_z, up, own=False):
+        device = (group, ((z + 1 if up else z - 1) * 2 + x) * 2 + core)
+        rows = key_rows(of_z, x, core, group)
+        return key_copy(rows, of_z if up else 4 + of_z, of_z, device, own)
+
+    def z_arrival(of_z):
+        return key_copy(key_rows(of_z, x, core, group), of_z, of_z, beside)
+
+    def x_copy(of_z, own=False):
+        return key_copy(key_rows(of_z, x, core, group), 8 + of_z, 8 + of_z, beside, own)
+
+    def x_arrival(of_z):
+        return key_copy(key_rows(of_z, 1 - x, core, group), 8 + of_z, 8 + of_z, beside)
+
+    def y_copy(of_z, of_x):
+        sem = 16 + of_z * 2 + of_x
+        return key_copy(key_rows(of_z, of_x, core, group), sem, sem, across)
+
+    def y_arrival(of_z, of_x):
+        sem = 16 + of_z * 2 + of_x
+        return key_copy(key_rows(of_z, of_x, core, 1 - group), sem, sem, across)
+
+    def sibling_copy(of_z, of_x, far, of_core=core):
+        sem = 24 + (of_z * 2 + of_x) * 2 + far
+        rows = key_rows(of_z, of_x, of_core, 1 - group if far else group)
+        return key_copy(rows, sem, sem, sibling)
+
+    def sibling_arrival(of_z, of_x, far):
+        return sibling_copy(of_z, of_x, far, 1 - core)
+
+    def hand_on(of_z, up):
+        z_arrival(of_z).wait_recv()
+
+        @pl.when(z < LAYERS - 1 if up else z > 0)
+        def _():
+            z_copy(of_z, up).start()
+
+        x_copy(of_z).start()
+        y_copy(of_z, x).start()
+        sibling_copy(of_z, x, 0).start()
 
     def own_copy(owner):
         return pltpu.make_async_remote_copy(
             src_ref=k_ref,
             dst_ref=key.at[pl.ds(pl.multiple_of(owner * 2 * half, 2 * half), 2 * half)],
-            send_sem=ks_sem.at[28],
-            recv_sem=kr_sem.at[28],
+            send_sem=ks_sem.at[40],
+            recv_sem=kr_sem.at[40],
             device_id=sibling,
             device_id_type=MESH,
         )
@@ -264,7 +261,16 @@
 
     start_all(g_send, g_recv, gs_sem, gr_sem)
     loads[1].wait()
-    ring_copy(0).start()
+
+    @pl.when(z < LAYERS - 1)
+    def _():
+        z_copy(z, True, own=True).start()
+
+    @pl.when(z > 0)
+    def _():
+        z_copy(z, False, own=True).start()
+
+    x_copy(z, own=True).start()
     own_copy(me).start()
     g_recv[rows_of(me), :] = g_send[rows_of(me), :]
     loads[2].wait()
@@ -274,8 +280,9 @@
         at = pl.ds(pl.multiple_of(t * COLUMNS, COLUMNS), COLUMNS)
         x_send[:, at] = matmul(place_t_ref[...], x_ref[:, at]).astype(jnp.bfloat16)
 
-    x_queue = [(x_send, x_recv, xs_sem, xr_sem, i) for i in range(1, n)]
-    part_queue = [(part, returned, ps_sem, pr_sem, i) for i in range(1, n)]
+    far_first = sorted(range(1, n), key=lambda i: abs(i - n // 2))
+    x_queue = [(x_send, x_recv, xs_sem, xr_sem, i) for i in far_first]
+    part_queue = [(part, returned, ps_sem, pr_sem, i) for i in far_first]
     queue = x_queue + part_queue
 
     def start_some(count):
@@ -302,16 +309,27 @@
 
     returned[rows_of(me), :] = part[rows_of(me), :]
 
-    steps = RING - 1
-    for s in range(steps):
-        ring_arrival(s).wait_recv()
-        if s + 1 < steps:
-            ring_copy(s + 1).start()
-        across_copy(s).start()
-        sibling_copy(s, False).start()
-        if s:
-            across_arrival(s - 1).wait_recv()
-            sibling_copy(s - 1, True).start()
+    for d in range(1, LAYERS):
+
+        @pl.when(z >= d)
+        def _():
+            hand_on(z - d, True)
+
+        @pl.when(z + d < LAYERS)
+        def _():
+            hand_on(z + d, False)
+
+        start_some(EACH)
+    layers = [(z + d) % LAYERS for d in range(LAYERS)]
+    for of_z in layers:
+        x_arrival(of_z).wait_recv()
+        y_copy(of_z, 1 - x).start()
+        sibling_copy(of_z, 1 - x, 0).start()
+        start_some(EACH)
+    others = [(of_z, x) for of_z in layers[1:]] + [(of_z, 1 - x) for of_z in layers]
+    for chip_at in others:
+        y_arrival(*chip_at).wait_recv()
+        sibling_copy(*chip_at, 1).start()
         start_some(EACH)
     start_some(2 * n)
 
@@ -331,12 +349,10 @@
         jnp.bfloat16
     )
 
-    across_arrival(steps - 1).wait_recv()
-    sibling_copy(steps - 1, True).start()
     own_copy(chip * 2 + 1 - core).wait_recv()
-    for s in range(steps):
-        sibling_arrival(s, False).wait_recv()
-        sibling_arrival(s, True).wait_recv()
+    for chip_at in others:
+        sibling_arrival(*chip_at, 0).wait_recv()
+        sibling_arrival(*chip_at, 1).wait_recv()
 
     @pl.loop(0, tiles)
     def _(t):
@@ -354,11 +370,32 @@
     wait_sent(x_send, x_recv, xs_sem, xr_sem)
     wait_sent(part, returned, ps_sem, pr_sem)
     own_copy(me).wait_send()
-    for s in range(steps):
-        ring_copy(s).wait_send()
-        across_copy(s).wait_send()
-        sibling_copy(s, False).wait_send()
-        sibling_copy(s, True).wait_send()
+
+    @pl.when(z < LAYERS - 1)
+    def _():
+        z_copy(z, True, own=True).wait_send()
+
+    @pl.when(z > 0)
+    def _():
+        z_copy(z, False, own=True).wait_send()
+
+    x_copy(z, own=True).wait_send()
+    for d in range(1, LAYERS):
+
+        @pl.when((z >= d) & (z < LAYERS - 1))
+        def _():
+            z_copy(z - d, True).wait_send()
+
+        @pl.when((z + d < LAYERS) & (z > 0))
+        def _():
+            z_copy(z + d, False).wait_send()
+
+    for of_z in layers[1:]:
+        x_copy(of_z).wait_send()
+    for chip_at in others:
+        y_copy(*chip_at).wait_send()
+        sibling_copy(*chip_at, 0).wait_send()
+        sibling_copy(*chip_at, 1).wait_send()
 
 
 def fused_shards(
@@ -396,7 +433,7 @@
             jax.ShapeDtypeStruct((width, held), jnp.bfloat16),
             jax.ShapeDtypeStruct((held, grad), jnp.bfloat16),
         ),
-        in_specs=[vmem] * 3 + [pl.BlockSpec(memory_space=pl.ANY)] * 5,
+        in_specs=[vmem] * 3 + [pl.BlockSpec(memory_space=pltpu.HBM)] * 5,
         out_specs=(vmem,) * 3,
         scratch_shapes=[
             pltpu.VMEM((total, width), jnp.bfloat16),
@@ -417,7 +454,7 @@
             pltpu.SemaphoreType.DMA((5,)),
         ]
         + [pltpu.SemaphoreType.DMA((holders,))] * 6
-        + [pltpu.SemaphoreType.DMA((29,))] * 2,
+        + [pltpu.SemaphoreType.DMA((41,))] * 2,
         compiler_params=pltpu.CompilerParams(
             collective_id=0, has_side_effects=True, vmem_limit_bytes=48 * 2**20
         ),
@@ -499,7 +536,7 @@
 
 
 def solution(mesh):
-    on_grid = mesh.shape["groups"] == 2 and mesh.shape["owner"] == 2 * RING
+    on_grid = mesh.shape["groups"] == 2 and mesh.shape["owner"] == 4 * LAYERS
     return jax.shard_map(
         fused_shards if on_grid else shards,
         mesh=mesh,

time: 148 us -> 136 us (0.919); the launches traced: 148 us -> 134 us
  Pallas kernels: 138 us -> 124 us
    pallas_call x1, Pallas kernels: 138 us -> 124 us  [fused_shards(): pl.pallas_call(functools.partial(fused_kernel, holders, cap), out_shape=(...]
where the time goes in v3:
time: 136 us; the launch traced here: 134 us
  Pallas kernels  124 us (91%)
  local copies, waits for them, and re-layouts  8.03 us (6%)
    pallas_call x1, Pallas kernels, fused_shards(): pl.pallas_call(functools.partial(fused_kernel, holders, cap), out_shape=(...  124 us
    unnamed x13, local copies, waits for them, and re-layouts  8.03 us

profile of v3, /device:TPU:27, one launch (start us, length us, event | category | flops | bytes accessed | tf_op | source)
XLA Modules:
  0.0 134.1 jit_solution(1223802520055821305)
XLA Ops:
  0.6 0.8 select_reduce_fusion
  1.4 0.2 convert_reduce_fusion
  1.6 0.1 compare_convert_fusion.local_ref
  1.7 0.1 fusion.place_ref
  1.8 0.0 copy-start
  1.8 1.2 copy-done
  3.0 0.0 copy-start.1
  3.0 1.2 copy-done.1
  4.3 0.0 copy-start.2
  4.3 1.0 copy-done.2
  5.3 0.0 copy-start.3
  5.3 0.9 copy-done.3
  6.3 0.0 copy-start.4
  6.3 0.9 copy-done.4
  7.2 124.2 %fused_backward.1 = (bf16[128,4096]{1,0:T(8,128)(2,1)S(1)}, bf16[4096,128]{1,0:T(8,128)(2,1)S(1)}, bf16[128,1024]{1,0:T(8,128)(2,1)S(1)}) custom-call(bf16[128,256]{1,0:T(8,128)(2,1)S(1)} %fusion.place_ref, bf16[256,128]{1,0:T(8,128)(2,1)S(1)} %fusion.1.place_t_ref, bf16[128,128]{1,0:T(8,128)(2,1)S(1)} %compare_convert_fusion.local_ref, ...), custom_call_target="tpu_custom_call" | custom-call | tf_op jit(solution)/shard_map/fused_backward/pallas_call | solution.py:429
  131.5 1.0 copy.13
  132.4 1.0 copy.14
  133.4 0.7 copy.15
  (3 shorter events, 0.0 us)
Async XLA Ops:
  1.8 1.2 copy-start
  3.0 1.2 copy-start.1
  4.3 1.0 copy-start.2
  5.3 0.9 copy-start.3
  6.3 0.9 copy-start.4
